TPU v7x, 32 devices: a whole 2x2x4 slice. The times are simulated.
32 devices in a mesh: runs: 2 (over y), tag: 8 (over z, x), strip: 2 (over core).
Axes of the slice: x: 2, y: 2, z: 4, core: 2. Of those that a mesh axis runs over, the one named last changes fastest.
Arguments:
- tracer: float32 [32, 128, 2048], P(('runs', 'tag'), 'strip'), parts along dimension 0, may hold values from 0.1 to 3
- water_depth: float32 [256, 2048], P(('runs', 'strip'), 'tag'), parts along dimension 0, may hold values from 1 to 3
- flow_east: float32 [256, 2048], P(('runs', 'strip'), 'tag'), parts along dimension 0, may hold values from -0.5 to 0.5
- flow_south: float32 [256, 2048], P(('runs', 'strip'), 'tag'), parts along dimension 0, may hold values from -0.5 to 0.5
- bed_level: float32 [128, 2048], P('strip', 'tag'), may hold values from 0 to 1
- wet_mask: int32 [256, 2048], P(('runs', 'strip')), parts along dimension 0, may hold values 0 or 1
- land_codes: int32 [128, 2048], P('strip'), may hold values from 0 to 3
- outfall: int32 [16], replicated, may hold values from 0 to 262143
- outfall_loads: float32 [32], P('runs'), parts along dimension 0, may hold values from 2 to 20
Outputs:
- tracer_next: float32 [32, 128, 2048], P(('runs', 'tag'), 'strip'), parts along dimension 0
- depth_next: float32 [256, 2048], P(('runs', 'strip'), 'tag'), parts along dimension 0
- east_next: float32 [256, 2048], P(('runs', 'strip'), 'tag'), parts along dimension 0
- south_next: float32 [256, 2048], P(('runs', 'strip'), 'tag'), parts along dimension 0
There are 2 independent parts, one for each index of `runs`. A program takes and returns all parts, laid end to end along the dimension named above; an argument that names none is the same for every part. Nothing has to cross between parts.
Inputs may be any that keep to these rules, and one draw needn't show every extreme that they name: `wet_mask`: 1 marks a wet cell. `land_codes`: 0 open water, 1 quay wall, 2 beach, 3 river mouth. `outfall`: flat cell index row * 2048 + column inside the window.
All inputs are finite; a program needn't handle non-finite values. No bound on the sum of `wet_mask` on one device may be relied on, other than what follows from the above.
Results may differ from a plain program's by a relative error of at most 0.00012.
Values sent between devices are 32-bit elements; how exact they have to be, the bound alone decides.
A program may use at most 64 MiB of HBM per device.

v0:
```python
import jax
import jax.numpy as jnp
from jax import lax
from jax.sharding import PartitionSpec as P

COLUMNS = 2048
SUBSTEPS = 4


STEP_RATIO = 0.2
GRAVITY_STEP = 0.1
COURANT = 0.2
DECAY_RATE = 0.005
SOURCE_STEP = 0.25
FRICTION_TABLE = (0.0, 0.3, 1.0, 2.5)
DISPERSION_TABLE = (0.02, 0.05, 0.08, 0.1)


def extended(cells, sides, width):
    for axis, dim in sides:
        count = lax.axis_size(axis)
        ends = count - 1
        head = lax.slice_in_dim(cells, 0, width, axis=dim)
        tail = lax.slice_in_dim(cells, cells.shape[dim] - width, cells.shape[dim], axis=dim)
        cells = jnp.concatenate(
            [
                lax.ppermute(tail, axis, [(i, (i + 1) % count) for i in range(ends)]),
                cells,
                lax.ppermute(head, axis, [((i + 1) % count, i) for i in range(ends)]),
            ],
            axis=dim,
        )
    return cells


def lookup(land_codes, lookup_table):
    result = jnp.zeros(land_codes.shape, jnp.float32)
    for code_value in range(4):
        result = result + jnp.where(land_codes == code_value, lookup_table[code_value], 0.0)
    return result


def shallow_step(padded, land_codes):
    water_depth = padded[0, 1:-1, 1:-1]
    surface = padded[0] + padded[3]
    flow_east = padded[1]
    flow_south = padded[2]
    divergence = 0.5 * (flow_east[1:-1, 2:] - flow_east[1:-1, :-2]) + 0.5 * (
        flow_south[2:, 1:-1] - flow_south[:-2, 1:-1]
    )
    depth_next = water_depth - STEP_RATIO * divergence
    friction = 1.0 + lookup(land_codes, FRICTION_TABLE)
    slope_east = 0.5 * (surface[1:-1, 2:] - surface[1:-1, :-2])
    slope_south = 0.5 * (surface[2:, 1:-1] - surface[:-2, 1:-1])
    east_next = (flow_east[1:-1, 1:-1] - GRAVITY_STEP * water_depth * slope_east) / friction
    south_next = (flow_south[1:-1, 1:-1] - GRAVITY_STEP * water_depth * slope_south) / friction
    return (depth_next, east_next, south_next)


def releases(outfall, outfall_loads, row_start, col_start, rows_here, cols_here):
    row_ids = outfall // COLUMNS - row_start
    col_ids = outfall % COLUMNS - col_start
    row_hit = lax.broadcasted_iota(jnp.int32, (1, rows_here, 1), 1) == row_ids[:, None, None]
    col_hit = lax.broadcasted_iota(jnp.int32, (1, 1, cols_here), 2) == col_ids[:, None, None]
    return jnp.where(row_hit & col_hit, SOURCE_STEP * outfall_loads[:, None, None], 0.0)


def summed_releases(outfall, outfall_loads, row_start, rows_here, cols_here):
    row_ids = outfall // COLUMNS - row_start
    col_ids = outfall % COLUMNS
    row_table = (lax.broadcasted_iota(jnp.int32, (rows_here, 1), 0) == row_ids[None, :]).astype(
        jnp.float32
    )
    col_table = jnp.where(
        lax.broadcasted_iota(jnp.int32, (1, cols_here), 1) == col_ids[:, None],
        SOURCE_STEP * outfall_loads[:, None],
        0.0,
    )
    return jnp.dot(
        row_table, col_table, precision=lax.Precision.HIGHEST, preferred_element_type=jnp.float32
    )


def advance(padded, tracer, speed_east, speed_south, dispersion, wet_cells, source, total_tracer):
    west_side = padded[:, 1:-1, :-2]
    east_side = padded[:, 1:-1, 2:]
    north_side = padded[:, :-2, 1:-1]
    south_side = padded[:, 2:, 1:-1]
    east_going = jnp.maximum(speed_east, 0.0)
    west_going = jnp.minimum(speed_east, 0.0)
    south_going = jnp.maximum(speed_south, 0.0)
    north_going = jnp.minimum(speed_south, 0.0)
    advected = (
        tracer
        - COURANT * (east_going * (tracer - west_side) + west_going * (east_side - tracer))
        - COURANT * (south_going * (tracer - north_side) + north_going * (south_side - tracer))
        + dispersion * (west_side + east_side + north_side + south_side - 4.0 * tracer)
    )
    return wet_cells * (advected + source) / (1.0 + DECAY_RATE * total_tracer)


def padded_rows(tracer):
    padded_tracer = extended(tracer, (("strip", 1),), 1)
    return jnp.pad(padded_tracer, ((0, 0), (0, 0), (1, 1)))


def shards(
    tracer,
    water_depth,
    flow_east,
    flow_south,
    bed_level,
    wet_mask,
    land_codes,
    outfall,
    outfall_loads,
):
    rows_here = water_depth.shape[0]
    tile_cols = water_depth.shape[1]
    tags_here = tracer.shape[0]
    tag_place = lax.axis_index("tag")
    strip_place = lax.axis_index("strip")
    col_start = tag_place * tile_cols
    row_start = strip_place * rows_here
    codes_tile = lax.dynamic_slice_in_dim(land_codes, col_start, tile_cols, 1)
    wet_tile = lax.dynamic_slice_in_dim(wet_mask, col_start, tile_cols, 1).astype(jnp.float32)
    stacked = jnp.stack([water_depth, flow_east, flow_south, bed_level])
    padded = extended(stacked, (("tag", 2), ("strip", 1)), 1)
    depth_next, east_next, south_next = shallow_step(padded, codes_tile)
    speeds = jnp.stack([wet_tile * east_next / depth_next, wet_tile * south_next / depth_next])
    gathered = lax.all_gather(speeds, "tag", axis=2, tiled=True)
    wet_cells = wet_mask.astype(jnp.float32)
    dispersion = lookup(land_codes, DISPERSION_TABLE)
    own_outfall = lax.dynamic_slice_in_dim(outfall, tag_place * tags_here, tags_here)
    own_loads = lax.dynamic_slice_in_dim(outfall_loads, tag_place * tags_here, tags_here)
    source = releases(own_outfall, own_loads, row_start, 0, rows_here, tracer.shape[2])
    total_now = lax.psum(jnp.sum(tracer, axis=0), "tag")
    source_total = summed_releases(outfall, outfall_loads, row_start, rows_here, tracer.shape[2])[
        None
    ]
    for substep in range(SUBSTEPS):
        padded_tracer = padded_rows(tracer)
        tracer = advance(
            padded_tracer,
            tracer,
            gathered[0],
            gathered[1],
            dispersion,
            wet_cells,
            source,
            total_now,
        )
        if substep + 1 < SUBSTEPS:
            padded_total = extended(total_now[None], (("strip", 1),), 1)
            padded_total = jnp.pad(padded_total, ((0, 0), (0, 0), (1, 1)))
            total_now = advance(
                padded_total,
                total_now[None],
                gathered[0],
                gathered[1],
                dispersion,
                wet_cells,
                source_total,
                total_now,
            )[0]
    return (tracer, depth_next, east_next, south_next)


def solution(mesh):
    in_specs = (
        P(("runs", "tag"), "strip", None),
        P(("runs", "strip"), "tag"),
        P(("runs", "strip"), "tag"),
        P(("runs", "strip"), "tag"),
        P("strip", "tag"),
        P(("runs", "strip"), None),
        P("strip", None),
        P(),
        P("runs"),
    )
    out_specs = (
        P(("runs", "tag"), "strip", None),
        P(("runs", "strip"), "tag"),
        P(("runs", "strip"), "tag"),
        P(("runs", "strip"), "tag"),
    )
    return jax.shard_map(shards, mesh=mesh, in_specs=in_specs, out_specs=out_specs, check_vma=False)
```

profile of v0, /device:TPU:1, one launch (start us, length us, event | category | flops | bytes accessed | tf_op | source)
XLA Modules:
  0.0 181.3 jit_solution(1289151793611240104)
XLA Ops:
  8.3 1.3 collective-permute-start.4
  9.6 3.0 %collective-permute-start.5 = (f32[2,1,2048]{2,1,0:T(1,128)S(1)}, f32[2,1,2048]{2,1,0:T(1,128)S(1)}, u32[]{:S(2)}, u32[]{:S(2)}) collective-permute-start(f32[2,1,2048]{2,1,0:T(1,128)S(1)} %get-tuple-element.27), channel_id=1, source_target_pairs={{1,0},{3,2},{5,4},{7,6},{9,8},{11,10},{13,12},{15,14},{17,16},{19,... | collective-permute-start | bytes 49160 | tf_op jit(solution)/shard_map/ppermute | solution.py:29
  13.8 4.0 %collective-permute-start = (f32[4,64,1]{2,1,0:T(8,128)S(1)}, f32[4,64,1]{2,1,0:T(8,128)S(1)}, u32[]{:S(2)}, u32[]{:S(2)}) collective-permute-start(f32[4,64,1]{2,1,0:T(8,128)S(1)} %get-tuple-element.39), channel_id=1, source_target_pairs={{0,2},{2,4},{4,6},{6,8},{8,10},{10,12},{12,14},{1,3},{3,5},{5,7},{... | collective-permute-start | bytes 3080 | tf_op jit(solution)/shard_map/ppermute | solution.py:27
  17.7 1.3 collective-permute-start.1
  20.9 4.1 %collective-permute-done.1 = f32[4,64,1]{2,1,0:T(8,128)S(1)} collective-permute-done((f32[4,64,1]{2,1,0:T(8,128)S(1)}, f32[4,64,1]{2,1,0:T(8,128)S(1)}, u32[]{:S(2)}, u32[]{:S(2)}) %collective-permute-start.1) | collective-permute-done | bytes 1056 | tf_op jit(solution)/shard_map/ppermute | solution.py:29
  25.2 1.4 collective-permute-start.2
  26.6 3.0 %collective-permute-start.3 = (f32[4,1,258]{2,1,0:T(1,128)S(1)}, f32[4,1,258]{2,1,0:T(1,128)S(1)}, u32[]{:S(2)}, u32[]{:S(2)}) collective-permute-start(f32[4,1,258]{2,1,0:T(1,128)S(1)} %get-tuple-element.35), channel_id=1, source_target_pairs={{1,0},{3,2},{5,4},{7,6},{9,8},{11,10},{13,12},{15,14},{17,16},{19,... | collective-permute-start | bytes 12392 | tf_op jit(solution)/shard_map/ppermute | solution.py:29
  33.7 58.6 %all-reduce.9.cloned.1.call-done = f32[64,2048]{1,0:T(8,128)} async-done(((f32[64,2048]{1,0:T(8,128)}), f32[64,2048]{1,0:T(8,128)}) %all-reduce.9.cloned.1.call-update) | async-done | bytes 524304 | tf_op jit(solution)/shard_map/psum | solution.py:137
  93.2 1.3 collective-permute-start.8
  94.5 4.4 %collective-permute-start.9 = (f32[1,1,2048]{2,1,0:T(1,128)S(1)}, f32[1,1,2048]{2,1,0:T(1,128)S(1)}, u32[]{:S(2)}, u32[]{:S(2)}) collective-permute-start(f32[1,1,2048]{2,1,0:T(1,128)S(1)} %get-tuple-element.33), channel_id=1, source_target_pairs={{1,0},{3,2},{5,4},{7,6},{9,8},{11,10},{13,12},{15,14},{17,16},{19,... | collective-permute-start | bytes 24584 | tf_op jit(solution)/shard_map/ppermute | solution.py:29
  100.8 31.9 %all-gather.2.cloned.1.call-done = f32[2,64,2048]{2,1,0:T(8,128)} async-done(((f32[2,64,256]{2,1,0:T(8,128)}), f32[2,64,2048]{2,1,0:T(8,128)}) %all-gather.2.cloned.1.call-update) | async-done | bytes 1048592 | tf_op jit(solution)/shard_map/all_gather | solution.py:131
  132.7 3.4 %fusion.104 = (f32[64,2048]{1,0:T(8,128)S(1)}, f32[1,64,2048]{2,1,0:T(8,128)S(1)}) fusion(f32[64,2048]{1,0:T(8,128)} %all-reduce.9.cloned.1.call-done, f32[1,64,2048]{2,1,0:T(8,128)} %convolution_bitcast_fusion, s32[64,2048]{1,0:T(8,128)S(1)} %copy-done.1, f32[1,64,2048]{2,1,0:T(8,128)} %bitcast.54, f32[1,1,2048]{2,1,0:T(1,128)S(1)} %collective-permute-done.9, ...), kind=kLoop, calls=%fused_computation.144 | loop fusion | flops 6029312 | bytes 5783552 | tf_op jit(solution)/shard_map/div | solution.py:99
  136.1 1.3 collective-permute-start.12
  137.4 5.1 %collective-permute-start.13 = (f32[1,1,2048]{2,1,0:T(1,128)S(1)}, f32[1,1,2048]{2,1,0:T(1,128)S(1)}, u32[]{:S(2)}, u32[]{:S(2)}) collective-permute-start(f32[1,1,2048]{2,1,0:T(1,128)S(1)} %get-tuple-element.31), channel_id=1, source_target_pairs={{1,0},{3,2},{5,4},{7,6},{9,8},{11,10},{13,12},{15,14},{17,16},{19,... | collective-permute-start | bytes 24584 | tf_op jit(solution)/shard_map/ppermute | solution.py:29
  144.7 1.3 collective-permute-start.16
  146.0 3.0 %collective-permute-start.17 = (f32[1,1,2048]{2,1,0:T(1,128)S(1)}, f32[1,1,2048]{2,1,0:T(1,128)S(1)}, u32[]{:S(2)}, u32[]{:S(2)}) collective-permute-start(f32[1,1,2048]{2,1,0:T(1,128)S(1)} %get-tuple-element.29), channel_id=1, source_target_pairs={{1,0},{3,2},{5,4},{7,6},{9,8},{11,10},{13,12},{15,14},{17,16},{19,... | collective-permute-start | bytes 24584 | tf_op jit(solution)/shard_map/ppermute | solution.py:29
  151.0 1.4 fusion.2
  152.5 1.3 collective-permute-start.6
  153.8 3.0 %collective-permute-start.7 = (f32[2,1,2048]{2,1,0:T(1,128)S(1)}, f32[2,1,2048]{2,1,0:T(1,128)S(1)}, u32[]{:S(2)}, u32[]{:S(2)}) collective-permute-start(f32[2,1,2048]{2,1,0:T(1,128)S(1)} %get-tuple-element.25), channel_id=1, source_target_pairs={{1,0},{3,2},{5,4},{7,6},{9,8},{11,10},{13,12},{15,14},{17,16},{19,... | collective-permute-start | bytes 49160 | tf_op jit(solution)/shard_map/ppermute | solution.py:29
  158.1 1.4 fusion.4
  160.8 3.2 %collective-permute-start.11 = (f32[2,1,2048]{2,1,0:T(1,128)S(1)}, f32[2,1,2048]{2,1,0:T(1,128)S(1)}, u32[]{:S(2)}, u32[]{:S(2)}) collective-permute-start(f32[2,1,2048]{2,1,0:T(1,128)S(1)} %get-tuple-element.23), channel_id=1, source_target_pairs={{1,0},{3,2},{5,4},{7,6},{9,8},{11,10},{13,12},{15,14},{17,16},{19,... | collective-permute-start | bytes 49160 | tf_op jit(solution)/shard_map/ppermute | solution.py:29
  165.1 1.4 fusion.6
  167.8 3.0 %collective-permute-start.15 = (f32[2,1,2048]{2,1,0:T(1,128)S(1)}, f32[2,1,2048]{2,1,0:T(1,128)S(1)}, u32[]{:S(2)}, u32[]{:S(2)}) collective-permute-start(f32[2,1,2048]{2,1,0:T(1,128)S(1)} %get-tuple-element.21), channel_id=1, source_target_pairs={{1,0},{3,2},{5,4},{7,6},{9,8},{11,10},{13,12},{15,14},{17,16},{19,... | collective-permute-start | bytes 49160 | tf_op jit(solution)/shard_map/ppermute | solution.py:29
  172.1 2.4 %fusion.8 = f32[2,64,2048]{2,1,0:T(8,128)} fusion(f32[2,1,2048]{2,1,0:T(1,128)S(1)} %collective-permute-done.15, f32[2,64,2048]{2,1,0:T(8,128)S(1)} %fusion.6, f32[2,1,2048]{2,1,0:T(1,128)S(1)} %collective-permute-done.14, f32[2,66,2050]{2,1,0:T(8,128)S(1)} %select_maximum_fusion, f32[64,2048]{1,0:T(8,128)S(1)} %get-tuple-element.15, ...), kind=kLoop, calls=%fused_computation.23 | loop fusion | flops 7340032 | bytes 7901320 | tf_op jit(solution)/shard_map/div | solution.py:99
  (87 shorter events, 21.3 us)
Async XLA Ops:
  7.2 11.9 %copy-start = (f32[2,64,2048]{2,1,0:T(8,128)S(1)}, f32[2,64,2048]{2,1,0:T(8,128)}, u32[]{:S(2)}) copy-start(f32[2,64,2048]{2,1,0:T(8,128)} %param.9) | copy-start | bytes 3145732
  7.2 85.1 %all-reduce.9.cloned.1.call-start = ((), (), s32[]{:S(2)}) async-start(), calls=%async_computation.1 | async-start | bytes 1048576 | tf_op jit(solution)/shard_map/psum | solution.py:137
  8.3 134.3 %collective-permute-start.4 = (f32[2,1,2048]{2,1,0:T(1,128)S(1)}, f32[2,1,2048]{2,1,0:T(1,128)S(1)}, u32[]{:S(2)}, u32[]{:S(2)}) collective-permute-start(f32[2,1,2048]{2,1,0:T(1,128)S(1)} %get-tuple-element.26), channel_id=1, source_target_pairs={{0,1},{2,3},{4,5},{6,7},{8,9},{10,11},{12,13},{14,15},{16,17},{18,... | collective-permute-start | bytes 49160 | tf_op jit(solution)/shard_map/ppermute | solution.py:27
  9.6 133.0 %collective-permute-start.5 = (f32[2,1,2048]{2,1,0:T(1,128)S(1)}, f32[2,1,2048]{2,1,0:T(1,128)S(1)}, u32[]{:S(2)}, u32[]{:S(2)}) collective-permute-start(f32[2,1,2048]{2,1,0:T(1,128)S(1)} %get-tuple-element.27), channel_id=1, source_target_pairs={{1,0},{3,2},{5,4},{7,6},{9,8},{11,10},{13,12},{15,14},{17,16},{19,... | collective-permute-start | bytes 49160 | tf_op jit(solution)/shard_map/ppermute | solution.py:29
  13.6 11.4 %copy-start.7 = (f32[64,256]{1,0:T(8,128)S(1)}, f32[64,256]{1,0:T(8,128)}, u32[]{:S(2)}) copy-start(f32[64,256]{1,0:T(8,128)} %param.10) | copy-start | bytes 196612
  13.6 11.4 %copy-start.8 = (f32[64,256]{1,0:T(8,128)S(1)}, f32[64,256]{1,0:T(8,128)}, u32[]{:S(2)}) copy-start(f32[64,256]{1,0:T(8,128)} %param.13) | copy-start | bytes 196612
  13.8 7.1 %collective-permute-start = (f32[4,64,1]{2,1,0:T(8,128)S(1)}, f32[4,64,1]{2,1,0:T(8,128)S(1)}, u32[]{:S(2)}, u32[]{:S(2)}) collective-permute-start(f32[4,64,1]{2,1,0:T(8,128)S(1)} %get-tuple-element.39), channel_id=1, source_target_pairs={{0,2},{2,4},{4,6},{6,8},{8,10},{10,12},{12,14},{1,3},{3,5},{5,7},{... | collective-permute-start | bytes 3080 | tf_op jit(solution)/shard_map/ppermute | solution.py:27
  17.7 7.3 %collective-permute-start.1 = (f32[4,64,1]{2,1,0:T(8,128)S(1)}, f32[4,64,1]{2,1,0:T(8,128)S(1)}, u32[]{:S(2)}, u32[]{:S(2)}) collective-permute-start(f32[4,64,1]{2,1,0:T(8,128)S(1)} %get-tuple-element.40), channel_id=1, source_target_pairs={{2,0},{4,2},{6,4},{8,6},{10,8},{12,10},{14,12},{3,1},{5,3},{7,5},{... | collective-permute-start | bytes 3080 | tf_op jit(solution)/shard_map/ppermute | solution.py:29
  19.9 112.8 %all-gather.2.cloned.1.call-start = ((), (), s32[]{:S(2)}) async-start(), calls=%async_computation | async-start | bytes 1179648 | tf_op jit(solution)/shard_map/all_gather | solution.py:131
  25.2 5.7 %collective-permute-start.2 = (f32[4,1,258]{2,1,0:T(1,128)S(1)}, f32[4,1,258]{2,1,0:T(1,128)S(1)}, u32[]{:S(2)}, u32[]{:S(2)}) collective-permute-start(f32[4,1,258]{2,1,0:T(1,128)S(1)} %get-tuple-element.34), channel_id=1, source_target_pairs={{0,1},{2,3},{4,5},{6,7},{8,9},{10,11},{12,13},{14,15},{16,17},{18,... | collective-permute-start | bytes 12392 | tf_op jit(solution)/shard_map/ppermute | solution.py:27
  26.6 4.3 %collective-permute-start.3 = (f32[4,1,258]{2,1,0:T(1,128)S(1)}, f32[4,1,258]{2,1,0:T(1,128)S(1)}, u32[]{:S(2)}, u32[]{:S(2)}) collective-permute-start(f32[4,1,258]{2,1,0:T(1,128)S(1)} %get-tuple-element.35), channel_id=1, source_target_pairs={{1,0},{3,2},{5,4},{7,6},{9,8},{11,10},{13,12},{15,14},{17,16},{19,... | collective-permute-start | bytes 12392 | tf_op jit(solution)/shard_map/ppermute | solution.py:29
  31.9 67.1 %copy-start.11 = (f32[64,256]{1,0:T(8,128)}, f32[64,256]{1,0:T(8,128)S(1)}, u32[]{:S(2)}) copy-start(f32[64,256]{1,0:T(8,128)S(1)} %get-tuple-element.12) | copy-start | bytes 196612
  93.2 5.8 %collective-permute-start.8 = (f32[1,1,2048]{2,1,0:T(1,128)S(1)}, f32[1,1,2048]{2,1,0:T(1,128)S(1)}, u32[]{:S(2)}, u32[]{:S(2)}) collective-permute-start(f32[1,1,2048]{2,1,0:T(1,128)S(1)} %get-tuple-element.32), channel_id=1, source_target_pairs={{0,1},{2,3},{4,5},{6,7},{8,9},{10,11},{12,13},{14,15},{16,17},{18,... | collective-permute-start | bytes 24584 | tf_op jit(solution)/shard_map/ppermute | solution.py:27
  94.5 5.2 %collective-permute-start.9 = (f32[1,1,2048]{2,1,0:T(1,128)S(1)}, f32[1,1,2048]{2,1,0:T(1,128)S(1)}, u32[]{:S(2)}, u32[]{:S(2)}) collective-permute-start(f32[1,1,2048]{2,1,0:T(1,128)S(1)} %get-tuple-element.33), channel_id=1, source_target_pairs={{1,0},{3,2},{5,4},{7,6},{9,8},{11,10},{13,12},{15,14},{17,16},{19,... | collective-permute-start | bytes 24584 | tf_op jit(solution)/shard_map/ppermute | solution.py:29
  136.1 7.0 %collective-permute-start.12 = (f32[1,1,2048]{2,1,0:T(1,128)S(1)}, f32[1,1,2048]{2,1,0:T(1,128)S(1)}, u32[]{:S(2)}, u32[]{:S(2)}) collective-permute-start(f32[1,1,2048]{2,1,0:T(1,128)S(1)} %get-tuple-element.30), channel_id=1, source_target_pairs={{0,1},{2,3},{4,5},{6,7},{8,9},{10,11},{12,13},{14,15},{16,17},{18,... | collective-permute-start | bytes 24584 | tf_op jit(solution)/shard_map/ppermute | solution.py:27
  137.4 6.0 %collective-permute-start.13 = (f32[1,1,2048]{2,1,0:T(1,128)S(1)}, f32[1,1,2048]{2,1,0:T(1,128)S(1)}, u32[]{:S(2)}, u32[]{:S(2)}) collective-permute-start(f32[1,1,2048]{2,1,0:T(1,128)S(1)} %get-tuple-element.31), channel_id=1, source_target_pairs={{1,0},{3,2},{5,4},{7,6},{9,8},{11,10},{13,12},{15,14},{17,16},{19,... | collective-permute-start | bytes 24584 | tf_op jit(solution)/shard_map/ppermute | solution.py:29
  144.7 4.4 %collective-permute-start.16 = (f32[1,1,2048]{2,1,0:T(1,128)S(1)}, f32[1,1,2048]{2,1,0:T(1,128)S(1)}, u32[]{:S(2)}, u32[]{:S(2)}) collective-permute-start(f32[1,1,2048]{2,1,0:T(1,128)S(1)} %get-tuple-element.28), channel_id=1, source_target_pairs={{0,1},{2,3},{4,5},{6,7},{8,9},{10,11},{12,13},{14,15},{16,17},{18,... | collective-permute-start | bytes 24584 | tf_op jit(solution)/shard_map/ppermute | solution.py:27
  146.0 3.8 %collective-permute-start.17 = (f32[1,1,2048]{2,1,0:T(1,128)S(1)}, f32[1,1,2048]{2,1,0:T(1,128)S(1)}, u32[]{:S(2)}, u32[]{:S(2)}) collective-permute-start(f32[1,1,2048]{2,1,0:T(1,128)S(1)} %get-tuple-element.29), channel_id=1, source_target_pairs={{1,0},{3,2},{5,4},{7,6},{9,8},{11,10},{13,12},{15,14},{17,16},{19,... | collective-permute-start | bytes 24584 | tf_op jit(solution)/shard_map/ppermute | solution.py:29
  152.5 4.3 %collective-permute-start.6 = (f32[2,1,2048]{2,1,0:T(1,128)S(1)}, f32[2,1,2048]{2,1,0:T(1,128)S(1)}, u32[]{:S(2)}, u32[]{:S(2)}) collective-permute-start(f32[2,1,2048]{2,1,0:T(1,128)S(1)} %get-tuple-element.24), channel_id=1, source_target_pairs={{0,1},{2,3},{4,5},{6,7},{8,9},{10,11},{12,13},{14,15},{16,17},{18,... | collective-permute-start | bytes 49160 | tf_op jit(solution)/shard_map/ppermute | solution.py:27
  153.8 3.9 %collective-permute-start.7 = (f32[2,1,2048]{2,1,0:T(1,128)S(1)}, f32[2,1,2048]{2,1,0:T(1,128)S(1)}, u32[]{:S(2)}, u32[]{:S(2)}) collective-permute-start(f32[2,1,2048]{2,1,0:T(1,128)S(1)} %get-tuple-element.25), channel_id=1, source_target_pairs={{1,0},{3,2},{5,4},{7,6},{9,8},{11,10},{13,12},{15,14},{17,16},{19,... | collective-permute-start | bytes 49160 | tf_op jit(solution)/shard_map/ppermute | solution.py:29
  159.5 4.5 %collective-permute-start.10 = (f32[2,1,2048]{2,1,0:T(1,128)S(1)}, f32[2,1,2048]{2,1,0:T(1,128)S(1)}, u32[]{:S(2)}, u32[]{:S(2)}) collective-permute-start(f32[2,1,2048]{2,1,0:T(1,128)S(1)} %get-tuple-element.22), channel_id=1, source_target_pairs={{0,1},{2,3},{4,5},{6,7},{8,9},{10,11},{12,13},{14,15},{16,17},{18,... | collective-permute-start | bytes 49160 | tf_op jit(solution)/shard_map/ppermute | solution.py:27
  160.8 3.9 %collective-permute-start.11 = (f32[2,1,2048]{2,1,0:T(1,128)S(1)}, f32[2,1,2048]{2,1,0:T(1,128)S(1)}, u32[]{:S(2)}, u32[]{:S(2)}) collective-permute-start(f32[2,1,2048]{2,1,0:T(1,128)S(1)} %get-tuple-element.23), channel_id=1, source_target_pairs={{1,0},{3,2},{5,4},{7,6},{9,8},{11,10},{13,12},{15,14},{17,16},{19,... | collective-permute-start | bytes 49160 | tf_op jit(solution)/shard_map/ppermute | solution.py:29
  166.5 4.3 %collective-permute-start.14 = (f32[2,1,2048]{2,1,0:T(1,128)S(1)}, f32[2,1,2048]{2,1,0:T(1,128)S(1)}, u32[]{:S(2)}, u32[]{:S(2)}) collective-permute-start(f32[2,1,2048]{2,1,0:T(1,128)S(1)} %get-tuple-element.20), channel_id=1, source_target_pairs={{0,1},{2,3},{4,5},{6,7},{8,9},{10,11},{12,13},{14,15},{16,17},{18,... | collective-permute-start | bytes 49160 | tf_op jit(solution)/shard_map/ppermute | solution.py:27
  167.8 3.9 %collective-permute-start.15 = (f32[2,1,2048]{2,1,0:T(1,128)S(1)}, f32[2,1,2048]{2,1,0:T(1,128)S(1)}, u32[]{:S(2)}, u32[]{:S(2)}) collective-permute-start(f32[2,1,2048]{2,1,0:T(1,128)S(1)} %get-tuple-element.21), channel_id=1, source_target_pairs={{1,0},{3,2},{5,4},{7,6},{9,8},{11,10},{13,12},{15,14},{17,16},{19,... | collective-permute-start | bytes 49160 | tf_op jit(solution)/shard_map/ppermute | solution.py:29
  (10 other events, 72.8 us)
Sparse Core Ops, SparseCore 0:
  20.1 72.1 all-reduce.8
  94.5 38.1 all-gather.1
where the time goes:
time: 182 us; the launch traced here: 181 us
  waiting for transfers between devices  99.3 us (55%)
  starting transfers between devices  43.7 us (24%)
  other arithmetic  20.3 us (11%)
  between operations  14.6 us (8%)
  local copies, waits for them, and re-layouts  2.28 us (1%)
    psum x1, waiting for transfers between devices, shards(): total_now = lax.psum(jnp.sum(tracer, axis=0), 'tag')  58.6 us
    all_gather x1, waiting for transfers between devices, shards(): gathered = lax.all_gather(speeds, 'tag', axis=2, tiled=True)  31.9 us
    ppermute x9, starting transfers between devices, extended(): lax.ppermute(head, axis, [((i + 1) % count, i) for i in range(ends)])  29.2 us
    ppermute x9, starting transfers between devices, extended(): lax.ppermute(tail, axis, [(i, (i + 1) % count) for i in range(ends)])  14.4 us
    div x7, other arithmetic, advance(): return wet_cells * (advected + source) / (1.0 + DECAY_RATE * total_tracer)  11.8 us
    ppermute x9, waiting for transfers between devices, extended(): lax.ppermute(head, axis, [((i + 1) % count, i) for i in range(ends)])  8.06 us
    concatenate x8, other arithmetic, extended(): jnp.concatenate([lax.ppermute(tail, axis, [(i, (i + 1) % count) for i in...  3.68 us
  transfers between devices with their start and end apart: 20, of which 10 were waited for; matrix products, arithmetic and copies ran while one was open for 7% of the time, Pallas kernels for 0%

commit v1 on v0

--- a/solution.py
+++ b/solution.py
@@ -1,10 +1,14 @@
+import functools
 import jax
 import jax.numpy as jnp
 from jax import lax
+from jax.experimental import pallas as pl
+from jax.experimental.pallas import tpu as pltpu
 from jax.sharding import PartitionSpec as P
 
 COLUMNS = 2048
 SUBSTEPS = 4
+MESH = pl.DeviceIdType.MESH
 
 
 STEP_RATIO = 0.2
@@ -166,6 +170,420 @@
     return (tracer, depth_next, east_next, south_next)
 
 
+def pick(codes, table):
+    return jnp.where(
+        codes == 0,
+        table[0],
+        jnp.where(codes == 1, table[1], jnp.where(codes == 2, table[2], table[3])),
+    )
+
+
+def flood_kernel(
+    n_tag,
+    tracer_ref,
+    depth_ref,
+    east_ref,
+    south_ref,
+    bed_ref,
+    wet_ref,
+    code_ref,
+    outfall_ref,
+    loads_ref,
+    tracer_out,
+    depth_out,
+    east_out,
+    south_out,
+    cols_out,
+    cols_in,
+    rows_out,
+    rows_in,
+    part,
+    from_x,
+    red,
+    from_z,
+    speeds,
+    totals,
+    coef,
+    wet_cells,
+    release,
+    field,
+    edge_out,
+    edge_in,
+    halo_send,
+    halo_recv,
+    x_send,
+    x_recv,
+    z_send,
+    z_recv,
+    speed_send,
+    speed_recv,
+    total_send,
+    total_recv,
+    edge_send,
+    edge_recv,
+):
+    tags, rows, cols = tracer_ref.shape
+    tile = depth_ref.shape[1]
+    n_z = n_tag // 2
+    place = lax.axis_index("tag")
+    strip = lax.axis_index("strip")
+    z, x = place // 2, place % 2
+    other_x, other_strip = 1 - x, 1 - strip
+    partner = z * 2 + other_x
+    blocks = rows // 8
+
+    def peer(k):
+        result, bit = z, 1
+        while bit < n_z:
+            if k & bit:
+                result = result + bit - 2 * bit * ((result // bit) % 2)
+            bit *= 2
+        return result
+
+    def to(axis, index, src, dst, send, recv):
+        return pltpu.make_async_remote_copy(
+            src_ref=src,
+            dst_ref=dst,
+            send_sem=send,
+            recv_sem=recv,
+            device_id={axis: index},
+            device_id_type=MESH,
+        )
+
+    def span(slot):
+        return pl.ds(pl.multiple_of(slot * tile, tile), tile)
+
+    sent = []
+
+    def go(copy):
+        copy.start()
+        sent.append(copy)
+
+    barrier = pltpu.get_barrier_semaphore()
+    cols_in[...] = jnp.zeros_like(cols_in)
+    for k in range(1, n_tag):
+        pl.semaphore_signal(
+            barrier, inc=1, device_id={"tag": lax.rem(place + k, n_tag)}, device_id_type=MESH
+        )
+    pl.semaphore_signal(barrier, inc=1, device_id={"strip": other_strip}, device_id_type=MESH)
+
+    water = depth_ref[...]
+    east = east_ref[...]
+    south = south_ref[...]
+    surface = water + bed_ref[...]
+    first = lax.broadcasted_iota(jnp.int32, (rows, 128), 1) == 0
+    cols_out[0] = jnp.where(first, east[:, 0:1], surface[:, 0:1])
+    cols_out[1] = jnp.where(first, east[:, tile - 1 : tile], surface[:, tile - 1 : tile])
+    upper = strip == 0
+    edge_first = lax.broadcasted_iota(jnp.int32, (8, tile), 0) == 0
+    rows_out[...] = jnp.where(
+        edge_first,
+        jnp.where(upper, south[rows - 1 : rows], south[0:1]),
+        jnp.where(upper, surface[rows - 1 : rows], surface[0:1]),
+    )
+    edge_out[...] = jnp.zeros_like(edge_out)
+    for f in range(tags):
+        edge_out[0, f : f + 1, :] = jnp.where(
+            upper, tracer_ref[f, rows - 1 : rows, :], tracer_ref[f, 0:1, :]
+        )
+    for slot in range(n_tag):
+        share = tracer_ref[0, :, slot * tile : (slot + 1) * tile]
+        for f in range(1, tags):
+            share = share + tracer_ref[f, :, slot * tile : (slot + 1) * tile]
+        part[slot % 2, slot // 2] = share
+
+    pl.semaphore_wait(barrier, n_tag)
+
+    to_west = to("tag", place - 1, cols_out.at[0], cols_in.at[1], halo_send.at[0], halo_recv.at[1])
+    to_east = to("tag", place + 1, cols_out.at[1], cols_in.at[0], halo_send.at[1], halo_recv.at[0])
+    to_strip = to("strip", other_strip, rows_out, rows_in, halo_send.at[2], halo_recv.at[2])
+
+    @pl.when(place > 0)
+    def _():
+        to_west.start()
+
+    @pl.when(place < n_tag - 1)
+    def _():
+        to_east.start()
+
+    go(to_strip)
+    for k in reversed(range(n_z)):
+        go(
+            to(
+                "tag",
+                partner,
+                part.at[other_x, peer(k)],
+                from_x.at[k],
+                x_send.at[k],
+                x_recv.at[k],
+            )
+        )
+    go(to("strip", other_strip, edge_out.at[0], edge_in.at[0], edge_send.at[0], edge_recv.at[0]))
+
+    @pl.when(place > 0)
+    def _():
+        to_east.wait_recv()
+
+    @pl.when(place < n_tag - 1)
+    def _():
+        to_west.wait_recv()
+
+    to_strip.wait_recv()
+    lane = lax.broadcasted_iota(jnp.int32, (rows, tile), 1)
+    row = lax.broadcasted_iota(jnp.int32, (rows, tile), 0)
+
+    def west_of(cells, edge):
+        return jnp.where(lane == 0, edge, pltpu.roll(cells, 1, 1))
+
+    def east_of(cells, edge):
+        return jnp.where(lane == tile - 1, edge, pltpu.roll(cells, tile - 1, 1))
+
+    def north_of(cells, edge):
+        return jnp.where(row == 0, jnp.where(upper, 0.0, edge), pltpu.roll(cells, 1, 0))
+
+    def south_of(cells, edge):
+        return jnp.where(row == rows - 1, jnp.where(upper, edge, 0.0), pltpu.roll(cells, rows - 1, 0))
+
+    west_in, east_in, strip_in = cols_in[0], cols_in[1], rows_in[...]
+    divergence = 0.5 * (
+        east_of(east, east_in[:, 0:1]) - west_of(east, west_in[:, 0:1])
+    ) + 0.5 * (south_of(south, strip_in[0:1]) - north_of(south, strip_in[0:1]))
+    depth_next = water - STEP_RATIO * divergence
+    own_codes = code_ref[:, span(place)]
+    own_wet = wet_ref[:, span(place)].astype(jnp.float32)
+    friction = 1.0 + pick(own_codes, FRICTION_TABLE)
+    slope_east = 0.5 * (east_of(surface, east_in[:, 1:2]) - west_of(surface, west_in[:, 1:2]))
+    slope_south = 0.5 * (south_of(surface, strip_in[1:2]) - north_of(surface, strip_in[1:2]))
+    east_next = (east - GRAVITY_STEP * water * slope_east) / friction
+    south_next = (south - GRAVITY_STEP * water * slope_south) / friction
+    depth_out[...] = depth_next
+    east_out[...] = east_next
+    south_out[...] = south_next
+    speeds[place, 0] = own_wet * east_next / depth_next
+    speeds[place, 1] = own_wet * south_next / depth_next
+
+    def gather(held, send, recv):
+        for k in range(1, n_z):
+            go(to("tag", peer(k) * 2 + x, held.at[place], held.at[place], send.at[k], recv.at[place]))
+        go(to("tag", partner, held.at[place], held.at[place], send.at[0], recv.at[place]))
+
+    def arrived(held, send, recv, slot):
+        to("tag", partner, held.at[slot], held.at[slot], send.at[0], recv.at[slot]).wait_recv()
+
+    def pass_on(held, send, recv, k):
+        slot = peer(k) * 2 + x
+        arrived(held, send, recv, slot)
+        go(to("tag", partner, held.at[slot], held.at[slot], send.at[n_z - 1 + k], recv.at[slot]))
+
+    gather(speeds, speed_send, speed_recv)
+
+    for k in reversed(range(n_z)):
+        into = from_x.at[k]
+        to("tag", partner, into, into, x_send.at[k], x_recv.at[k]).wait_recv()
+        red[k] = part[x, peer(k)] + into[...]
+        if k:
+            go(to("tag", peer(k) * 2 + x, red.at[k], from_z.at[k], z_send.at[k], z_recv.at[k]))
+
+    def prepare(i, carry):
+        at = pl.multiple_of(i * 8, 8)
+        ids = (
+            (strip * rows + at + lax.broadcasted_iota(jnp.int32, (8, cols), 0)) * COLUMNS
+            + lax.broadcasted_iota(jnp.int32, (8, cols), 1)
+        )
+        for f in range(tags):
+            t = place * tags + f
+            release[f, pl.ds(at, 8), :] = jnp.where(
+                ids == outfall_ref[t], SOURCE_STEP * loads_ref[t], 0.0
+            )
+            field[0, f, pl.ds(at + 8, 8), :] = tracer_ref[f, pl.ds(at, 8), :]
+        all_tags = jnp.zeros((8, cols), jnp.float32)
+        for t in range(outfall_ref.shape[0]):
+            all_tags = all_tags + jnp.where(ids == outfall_ref[t], SOURCE_STEP * loads_ref[t], 0.0)
+        release[tags, pl.ds(at, 8), :] = all_tags
+        wet_cells[pl.ds(at, 8), :] = wet_ref[pl.ds(at, 8), :].astype(jnp.float32)
+        return carry
+
+    lax.fori_loop(0, blocks, prepare, 0)
+
+    own_total = red[0]
+    for k in range(1, n_z):
+        to("tag", partner, red.at[k], from_z.at[k], z_send.at[k], z_recv.at[k]).wait_recv()
+        own_total = own_total + from_z[k]
+    totals[place] = own_total
+    gather(totals, total_send, total_recv)
+
+    def weigh(slot):
+        go_east = speeds[slot, 0]
+        go_south = speeds[slot, 1]
+        spread = pick(code_ref[:, span(slot)], DISPERSION_TABLE)
+        west = spread + COURANT * jnp.maximum(go_east, 0.0)
+        east = spread - COURANT * jnp.minimum(go_east, 0.0)
+        north = spread + COURANT * jnp.maximum(go_south, 0.0)
+        south = spread - COURANT * jnp.minimum(go_south, 0.0)
+        coef[0, :, span(slot)] = 1.0 - ((west + east) + (north + south))
+        column = slot * tile + lane
+        coef[1, :, span(slot)] = jnp.where(column == 0, 0.0, west)
+        coef[2, :, span(slot)] = jnp.where(column == cols - 1, 0.0, east)
+        coef[3, :, span(slot)] = jnp.where((row == 0) & upper, 0.0, north)
+        coef[4, :, span(slot)] = jnp.where((row == rows - 1) & (strip == 1), 0.0, south)
+
+    def settle(slot):
+        field[0, tags, 8 : 8 + rows, span(slot)] = totals[slot]
+
+    weigh(place)
+    for k in range(1, n_z):
+        pass_on(speeds, speed_send, speed_recv, k)
+        weigh(peer(k) * 2 + x)
+    for k in range(n_z):
+        slot = peer(k) * 2 + other_x
+        arrived(speeds, speed_send, speed_recv, slot)
+        weigh(slot)
+        if k + 1 < n_z:
+            pass_on(totals, total_send, total_recv, k + 1)
+            settle(peer(k + 1) * 2 + x)
+    settle(place)
+    for k in range(n_z):
+        slot = peer(k) * 2 + other_x
+        arrived(totals, total_send, total_recv, slot)
+        settle(slot)
+
+    last = jnp.where(upper, blocks - 1, 0)
+
+    def edge_row(now, f):
+        return jnp.where(
+            upper, field[now, f, 7 + rows : 8 + rows, :], field[now, f, 8:9, :]
+        )
+
+    def exchange(n):
+        return to(
+            "strip", other_strip, edge_out.at[n], edge_in.at[n], edge_send.at[n], edge_recv.at[n]
+        )
+
+    edge_out[1, tags : tags + 1, :] = edge_row(0, tags)
+    go(exchange(1))
+
+    def put_halo(n, now, fields):
+        for f in fields:
+            got = edge_in[n, f : f + 1, :]
+            field[now, f, 7:8, :] = got
+            field[now, f, 8 + rows : 9 + rows, :] = got
+
+    exchange(0).wait_recv()
+    put_halo(0, 0, range(tags))
+    exchange(1).wait_recv()
+    put_halo(1, 0, [tags])
+
+    for substep in range(SUBSTEPS):
+        now, later = substep % 2, 1 - substep % 2
+        ends = substep == SUBSTEPS - 1
+        if substep:
+            exchange(substep + 1).wait_recv()
+            put_halo(substep + 1, now, range(tags + 1))
+
+        def block(i, carry):
+            at = pl.multiple_of(lax.rem(last + i, blocks) * 8, 8)
+            here = pl.ds(at, 8)
+            rate = wet_cells[here, :] / (1.0 + DECAY_RATE * field[now, tags, pl.ds(at + 8, 8), :])
+            for f in range(tags if ends else tags + 1):
+                wide = field[now, f, pl.ds(at, 24), :]
+                cell = wide[8:16]
+                value = (
+                    coef[0, here, :] * cell
+                    + coef[1, here, :] * pltpu.roll(cell, 1, 1)
+                    + coef[2, here, :] * pltpu.roll(cell, cols - 1, 1)
+                    + coef[3, here, :] * wide[7:15]
+                    + coef[4, here, :] * wide[9:17]
+                    + release[f, here, :]
+                ) * rate
+                if ends:
+                    tracer_out[f, here, :] = value
+                else:
+                    field[later, f, pl.ds(at + 8, 8), :] = value
+            if not ends:
+
+                @pl.when(i == 0)
+                def _():
+                    for f in range(tags + 1):
+                        edge_out[substep + 2, f : f + 1, :] = edge_row(later, f)
+                    exchange(substep + 2).start()
+
+            return carry
+
+        lax.fori_loop(0, blocks, block, 0)
+
+    for n in range(SUBSTEPS - 1):
+        exchange(n + 2).wait_send()
+    for copy in sent:
+        copy.wait_send()
+
+    @pl.when(place > 0)
+    def _():
+        to_west.wait_send()
+
+    @pl.when(place < n_tag - 1)
+    def _():
+        to_east.wait_send()
+
+
+def fused(n_tag, *arrays):
+    tracer, water = arrays[0], arrays[1]
+    tags, rows, cols = tracer.shape
+    tile = water.shape[1]
+    n_z = n_tag // 2
+    f32 = jnp.float32
+    dma = pltpu.SemaphoreType.DMA
+    vmem = pl.BlockSpec(memory_space=pltpu.VMEM)
+    smem = pl.BlockSpec(memory_space=pltpu.SMEM)
+    plane = jax.ShapeDtypeStruct(water.shape, f32)
+    return pl.pallas_call(
+        functools.partial(flood_kernel, n_tag),
+        out_shape=(jax.ShapeDtypeStruct(tracer.shape, f32), plane, plane, plane),
+        in_specs=[vmem] * 7 + [smem] * 2,
+        out_specs=(vmem,) * 4,
+        scratch_shapes=[
+            pltpu.VMEM((2, rows, 128), f32),
+            pltpu.VMEM((2, rows, 128), f32),
+            pltpu.VMEM((8, tile), f32),
+            pltpu.VMEM((8, tile), f32),
+            pltpu.VMEM((2, n_z, rows, tile), f32),
+            pltpu.VMEM((n_z, rows, tile), f32),
+            pltpu.VMEM((n_z, rows, tile), f32),
+            pltpu.VMEM((n_z, rows, tile), f32),
+            pltpu.VMEM((n_tag, 2, rows, tile), f32),
+            pltpu.VMEM((n_tag, rows, tile), f32),
+            pltpu.VMEM((5, rows, cols), f32),
+            pltpu.VMEM((rows, cols), f32),
+            pltpu.VMEM((tags + 1, rows, cols), f32),
+            pltpu.VMEM((2, tags + 1, rows + 16, cols), f32),
+            pltpu.VMEM((SUBSTEPS + 1, 8, cols), f32),
+            pltpu.VMEM((SUBSTEPS + 1, 8, cols), f32),
+            dma((3,)),
+            dma((3,)),
+            dma((n_z,)),
+            dma((n_z,)),
+            dma((n_z,)),
+            dma((n_z,)),
+            dma((2 * n_z - 1,)),
+            dma((n_tag,)),
+            dma((2 * n_z - 1,)),
+            dma((n_tag,)),
+            dma((SUBSTEPS + 1,)),
+            dma((SUBSTEPS + 1,)),
+        ],
+        compiler_params=pltpu.CompilerParams(
+            collective_id=0, has_side_effects=True, vmem_limit_bytes=48 * 1024 * 1024
+        ),
+    )(*arrays)
+
+
+def fits(n_tag, n_strip, tags, rows, cols):
+    tile = cols // n_tag
+    z_power = n_tag % 2 == 0 and (n_tag // 2) & (n_tag // 2 - 1) == 0
+    return (
+        n_strip == 2 and z_power and n_tag <= 16 and tile % 128 == 0 and rows % 8 == 0 and tags < 8
+    )
+
+
 def solution(mesh):
     in_specs = (
         P(("runs", "tag"), "strip", None),
@@ -184,4 +602,11 @@
         P(("runs", "strip"), "tag"),
         P(("runs", "strip"), "tag"),
     )
-    return jax.shard_map(shards, mesh=mesh, in_specs=in_specs, out_specs=out_specs, check_vma=False)
+
+    def local(*arrays):
+        n_tag, n_strip = mesh.shape["tag"], mesh.shape["strip"]
+        if fits(n_tag, n_strip, *arrays[0].shape):
+            return fused(n_tag, *arrays)
+        return shards(*arrays)
+
+    return jax.shard_map(local, mesh=mesh, in_specs=in_specs, out_specs=out_specs, check_vma=False)

time: 182 us -> 64.1 us (0.35)
  waiting for transfers between devices: 99.3 us -> 0 us
  Pallas kernels: 0 us -> 52.1 us
  starting transfers between devices: 43.7 us -> 0 us
  other arithmetic: 20.3 us -> 0 us
  between operations: 14.6 us -> 0.66 us
  local copies, waits for them, and re-layouts: 2.28 us -> 10.8 us
    psum x1 -> x0, waiting for transfers between devices: 58.6 us -> none  [shards(): total_now = lax.psum(jnp.sum(tracer, axis=0), 'tag')]
    pallas_call x0 -> x1, Pallas kernels: none -> 52.1 us  [fused(): pl.pallas_call(functools.partial(flood_kernel, n_tag), out_shape=(jax.Sha...]
    ppermute x18 -> x0, starting transfers between devices: 43.6 us -> none  [the longest x9 29.2 us: extended(): lax.ppermute(head, axis, [((i + 1) % count, i) for i in range(ends)])]
    all_gather x1 -> x0, waiting for transfers between devices: 31.9 us -> none  [shards(): gathered = lax.all_gather(speeds, 'tag', axis=2, tiled=True)]
    div x7 -> x0, other arithmetic: 11.8 us -> none  [advance(): return wet_cells * (advected + source) / (1.0 + DECAY_RATE * total_tracer)]
    unnamed x28 -> x22, local copies, waits for them, and re-layouts: 0.07 us -> 10.8 us
    ppermute x18 -> x0, waiting for transfers between devices: 8.75 us -> none  [the longest x9 8.06 us: extended(): lax.ppermute(head, axis, [((i + 1) % count, i) for i in range(ends)])]
    concatenate x8 -> x0, other arithmetic: 3.68 us -> none  [extended(): jnp.concatenate([lax.ppermute(tail, axis, [(i, (i + 1) % count) for i in...]
  transfers between devices with their start and end apart: 20 -> 0, of which waited for: 10 -> 0; matrix products, arithmetic and copies ran while one was open for 7% -> 0% of each run, Pallas kernels for 0% -> 0%
where the time goes in v1:
time: 64.1 us; the launch traced here: 63.6 us
  Pallas kernels  52.1 us (81%)
  local copies, waits for them, and re-layouts  10.8 us (17%)
  between operations  0.66 us (1%)
    pallas_call x1, Pallas kernels, fused(): pl.pallas_call(functools.partial(flood_kernel, n_tag), out_shape=(jax.Sha...  52.1 us
    unnamed x22, local copies, waits for them, and re-layouts  10.8 us

profile of v1, /device:TPU:1, one launch (start us, length us, event | category | flops | bytes accessed | tf_op | source)
XLA Modules:
  0.0 63.6 jit_solution(9599983197812055766)
XLA Ops:
  0.6 0.0 copy-start
  0.6 1.2 %copy-done = f32[2,64,2048]{2,1,0:T(8,128)S(1)} copy-done((f32[2,64,2048]{2,1,0:T(8,128)S(1)}, f32[2,64,2048]{2,1,0:T(8,128)}, u32[]{:S(2)}) %copy-start) | copy-done | bytes 1048600
  1.9 0.0 copy-start.1
  1.9 1.0 %copy-done.1 = s32[64,2048]{1,0:T(8,128)S(1)} copy-done((s32[64,2048]{1,0:T(8,128)S(1)}, s32[64,2048]{1,0:T(8,128)}, u32[]{:S(2)}) %copy-start.1) | copy-done | bytes 524312
  2.9 0.0 copy-start.2
  2.9 1.0 %copy-done.2 = s32[64,2048]{1,0:T(8,128)S(1)} copy-done((s32[64,2048]{1,0:T(8,128)S(1)}, s32[64,2048]{1,0:T(8,128)}, u32[]{:S(2)}) %copy-start.2) | copy-done | bytes 524312
  3.9 0.0 copy-start.3
  3.9 0.8 %copy-done.3 = f32[64,256]{1,0:T(8,128)S(1)} copy-done((f32[64,256]{1,0:T(8,128)S(1)}, f32[64,256]{1,0:T(8,128)}, u32[]{:S(2)}) %copy-start.3) | copy-done | bytes 65560
  4.8 0.0 copy-start.4
  4.8 0.8 %copy-done.4 = f32[64,256]{1,0:T(8,128)S(1)} copy-done((f32[64,256]{1,0:T(8,128)S(1)}, f32[64,256]{1,0:T(8,128)}, u32[]{:S(2)}) %copy-start.4) | copy-done | bytes 65560
  5.6 0.0 copy-start.5
  5.6 0.8 %copy-done.5 = f32[64,256]{1,0:T(8,128)S(1)} copy-done((f32[64,256]{1,0:T(8,128)S(1)}, f32[64,256]{1,0:T(8,128)}, u32[]{:S(2)}) %copy-start.5) | copy-done | bytes 65560
  6.5 0.0 copy-start.6
  6.5 0.8 %copy-done.6 = f32[64,256]{1,0:T(8,128)S(1)} copy-done((f32[64,256]{1,0:T(8,128)S(1)}, f32[64,256]{1,0:T(8,128)}, u32[]{:S(2)}) %copy-start.6) | copy-done | bytes 65560
  7.3 0.0 copy-start.7
  7.3 0.7 %copy-done.7 = s32[16]{0:T(128)S(1)} copy-done((s32[16]{0:T(128)S(1)}, s32[16]{0:T(128)}, u32[]{:S(2)}) %copy-start.7) | copy-done | bytes 88
  8.0 0.0 copy-start.8
  8.0 0.7 %copy-done.8 = f32[16]{0:T(128)S(1)} copy-done((f32[16]{0:T(128)S(1)}, f32[16]{0:T(128)}, u32[]{:S(2)}) %copy-start.8) | copy-done | bytes 88
  8.6 52.1 %shard_map.120 = (f32[2,64,2048]{2,1,0:T(8,128)S(1)}, f32[64,256]{1,0:T(8,128)S(1)}, f32[64,256]{1,0:T(8,128)S(1)}, f32[64,256]{1,0:T(8,128)S(1)}) custom-call(f32[2,64,2048]{2,1,0:T(8,128)S(1)} %copy-done, f32[64,256]{1,0:T(8,128)S(1)} %copy-done.3, f32[64,256]{1,0:T(8,128)S(1)} %copy-done.4, f32[64,256]{1,0:T(8,128)S(1)} %copy-done.5, ...), custom_call_target="tpu_custom_call" | custom-call | tf_op jit(solution)/shard_map/pallas_call | solution.py:538
  60.8 1.0 %copy.17 = f32[2,64,2048]{2,1,0:T(8,128)} copy(f32[2,64,2048]{2,1,0:T(8,128)S(1)} %get-tuple-element.8) | data formatting | bytes 2097152
  61.7 0.6 copy.18
  62.4 0.6 copy.19
  63.0 0.6 copy.20
Async XLA Ops:
  0.6 1.2 %copy-start = (f32[2,64,2048]{2,1,0:T(8,128)S(1)}, f32[2,64,2048]{2,1,0:T(8,128)}, u32[]{:S(2)}) copy-start(f32[2,64,2048]{2,1,0:T(8,128)} %tracer_ref.1) | copy-start | bytes 3145732
  1.9 1.0 %copy-start.1 = (s32[64,2048]{1,0:T(8,128)S(1)}, s32[64,2048]{1,0:T(8,128)}, u32[]{:S(2)}) copy-start(s32[64,2048]{1,0:T(8,128)} %wet_ref.1) | copy-start | bytes 1572868
  2.9 1.0 %copy-start.2 = (s32[64,2048]{1,0:T(8,128)S(1)}, s32[64,2048]{1,0:T(8,128)}, u32[]{:S(2)}) copy-start(s32[64,2048]{1,0:T(8,128)} %code_ref.1) | copy-start | bytes 1572868
  3.9 0.8 %copy-start.3 = (f32[64,256]{1,0:T(8,128)S(1)}, f32[64,256]{1,0:T(8,128)}, u32[]{:S(2)}) copy-start(f32[64,256]{1,0:T(8,128)} %depth_ref.1) | copy-start | bytes 196612
  4.8 0.8 %copy-start.4 = (f32[64,256]{1,0:T(8,128)S(1)}, f32[64,256]{1,0:T(8,128)}, u32[]{:S(2)}) copy-start(f32[64,256]{1,0:T(8,128)} %east_ref.1) | copy-start | bytes 196612
  5.6 0.8 %copy-start.5 = (f32[64,256]{1,0:T(8,128)S(1)}, f32[64,256]{1,0:T(8,128)}, u32[]{:S(2)}) copy-start(f32[64,256]{1,0:T(8,128)} %south_ref.1) | copy-start | bytes 196612
  6.5 0.8 %copy-start.6 = (f32[64,256]{1,0:T(8,128)S(1)}, f32[64,256]{1,0:T(8,128)}, u32[]{:S(2)}) copy-start(f32[64,256]{1,0:T(8,128)} %bed_ref.1) | copy-start | bytes 196612
  7.3 0.7 %copy-start.7 = (s32[16]{0:T(128)S(1)}, s32[16]{0:T(128)}, u32[]{:S(2)}) copy-start(s32[16]{0:T(128)} %outfall_ref.1) | copy-start | bytes 196
  8.0 0.7 %copy-start.8 = (f32[16]{0:T(128)S(1)}, f32[16]{0:T(128)}, u32[]{:S(2)}) copy-start(f32[16]{0:T(128)} %loads_ref.1) | copy-start | bytes 196

commit v2 on v1

--- a/solution.py
+++ b/solution.py
@@ -180,6 +180,19 @@
 
 def flood_kernel(
     n_tag,
+    tracer_hbm,
+    depth_hbm,
+    east_hbm,
+    south_hbm,
+    bed_hbm,
+    wet_hbm,
+    code_hbm,
+    outfall_hbm,
+    loads_hbm,
+    tracer_out,
+    depth_out,
+    east_out,
+    south_out,
     tracer_ref,
     depth_ref,
     east_ref,
@@ -189,10 +202,7 @@
     code_ref,
     outfall_ref,
     loads_ref,
-    tracer_out,
-    depth_out,
-    east_out,
-    south_out,
+    load_sem,
     cols_out,
     cols_in,
     rows_out,
@@ -259,6 +269,25 @@
         copy.start()
         sent.append(copy)
 
+    loads = [
+        pltpu.make_async_copy(src, dst, load_sem.at[n])
+        for n, (src, dst) in enumerate(
+            (
+                (depth_hbm, depth_ref),
+                (bed_hbm, bed_ref),
+                (east_hbm, east_ref),
+                (south_hbm, south_ref),
+                (tracer_hbm, tracer_ref),
+                (code_hbm, code_ref),
+                (wet_hbm, wet_ref),
+                (outfall_hbm, outfall_ref),
+                (loads_hbm, loads_ref),
+            )
+        )
+    ]
+    for load in loads:
+        load.start()
+
     barrier = pltpu.get_barrier_semaphore()
     cols_in[...] = jnp.zeros_like(cols_in)
     for k in range(1, n_tag):
@@ -267,6 +296,8 @@
         )
     pl.semaphore_signal(barrier, inc=1, device_id={"strip": other_strip}, device_id_type=MESH)
 
+    for load in loads[:4]:
+        load.wait()
     water = depth_ref[...]
     east = east_ref[...]
     south = south_ref[...]
@@ -282,6 +313,7 @@
         jnp.where(upper, surface[rows - 1 : rows], surface[0:1]),
     )
     edge_out[...] = jnp.zeros_like(edge_out)
+    loads[4].wait()
     for f in range(tags):
         edge_out[0, f : f + 1, :] = jnp.where(
             upper, tracer_ref[f, rows - 1 : rows, :], tracer_ref[f, 0:1, :]
@@ -329,6 +361,8 @@
         to_west.wait_recv()
 
     to_strip.wait_recv()
+    for load in loads[5:]:
+        load.wait()
     lane = lax.broadcasted_iota(jnp.int32, (rows, tile), 1)
     row = lax.broadcasted_iota(jnp.int32, (rows, tile), 0)
 
@@ -403,7 +437,10 @@
         wet_cells[pl.ds(at, 8), :] = wet_ref[pl.ds(at, 8), :].astype(jnp.float32)
         return carry
 
+    pass_on(speeds, speed_send, speed_recv, 1)
     lax.fori_loop(0, blocks, prepare, 0)
+    for k in range(2, n_z):
+        pass_on(speeds, speed_send, speed_recv, k)
 
     own_total = red[0]
     for k in range(1, n_z):
@@ -432,16 +469,15 @@
 
     weigh(place)
     for k in range(1, n_z):
-        pass_on(speeds, speed_send, speed_recv, k)
         weigh(peer(k) * 2 + x)
+    for k in range(1, n_z):
+        pass_on(totals, total_send, total_recv, k)
+        settle(peer(k) * 2 + x)
+    settle(place)
     for k in range(n_z):
         slot = peer(k) * 2 + other_x
         arrived(speeds, speed_send, speed_recv, slot)
         weigh(slot)
-        if k + 1 < n_z:
-            pass_on(totals, total_send, total_recv, k + 1)
-            settle(peer(k + 1) * 2 + x)
-    settle(place)
     for k in range(n_z):
         slot = peer(k) * 2 + other_x
         arrived(totals, total_send, total_recv, slot)
@@ -525,6 +561,15 @@
         to_east.wait_send()
 
 
+def store_kernel(*refs):
+    sem = refs[8]
+    copies = [pltpu.make_async_copy(refs[n], refs[4 + n], sem.at[n]) for n in range(4)]
+    for copy in copies:
+        copy.start()
+    for copy in copies:
+        copy.wait()
+
+
 def fused(n_tag, *arrays):
     tracer, water = arrays[0], arrays[1]
     tags, rows, cols = tracer.shape
@@ -533,14 +578,17 @@
     f32 = jnp.float32
     dma = pltpu.SemaphoreType.DMA
     vmem = pl.BlockSpec(memory_space=pltpu.VMEM)
-    smem = pl.BlockSpec(memory_space=pltpu.SMEM)
+    hbm = pl.BlockSpec(memory_space=pltpu.HBM)
     plane = jax.ShapeDtypeStruct(water.shape, f32)
-    return pl.pallas_call(
+    results = pl.pallas_call(
         functools.partial(flood_kernel, n_tag),
         out_shape=(jax.ShapeDtypeStruct(tracer.shape, f32), plane, plane, plane),
-        in_specs=[vmem] * 7 + [smem] * 2,
+        in_specs=[hbm] * 9,
         out_specs=(vmem,) * 4,
         scratch_shapes=[
+            *[pltpu.VMEM(a.shape, a.dtype) for a in arrays[:7]],
+            *[pltpu.SMEM(a.shape, a.dtype) for a in arrays[7:]],
+            dma((9,)),
             pltpu.VMEM((2, rows, 128), f32),
             pltpu.VMEM((2, rows, 128), f32),
             pltpu.VMEM((8, tile), f32),
@@ -571,9 +619,17 @@
             dma((SUBSTEPS + 1,)),
         ],
         compiler_params=pltpu.CompilerParams(
-            collective_id=0, has_side_effects=True, vmem_limit_bytes=48 * 1024 * 1024
+            collective_id=0, has_side_effects=True, vmem_limit_bytes=60 * 1024 * 1024
         ),
     )(*arrays)
+    return pl.pallas_call(
+        store_kernel,
+        out_shape=tuple(jax.ShapeDtypeStruct(r.shape, r.dtype) for r in results),
+        in_specs=[vmem] * 4,
+        out_specs=(hbm,) * 4,
+        scratch_shapes=[dma((4,))],
+        compiler_params=pltpu.CompilerParams(vmem_limit_bytes=60 * 1024 * 1024),
+    )(*results)
 
 
 def fits(n_tag, n_strip, tags, rows, cols):

time: 64.1 us -> 52.4 us (0.82)
  local copies, waits for them, and re-layouts: 10.8 us -> 0 us
  Pallas kernels: 52.1 us -> 51 us
    unnamed x22 -> x0, local copies, waits for them, and re-layouts: 10.8 us -> none
    pallas_call x1, Pallas kernels: 52.1 us -> 48.7 us  [fused(): pl.pallas_call(functools.partial(flood_kernel, n_tag), out_shape=(jax.Sha...]
    pallas_call x0 -> x1, Pallas kernels: none -> 2.32 us  [fused(): pl.pallas_call(store_kernel, out_shape=tuple((jax.ShapeDtypeStruct(r.shap...]
where the time goes in v2:
time: 52.4 us; the launch traced here: 51.7 us
  Pallas kernels  51 us (97%)
  between operations  0.64 us (1%)
    pallas_call x1, Pallas kernels, fused(): pl.pallas_call(functools.partial(flood_kernel, n_tag), out_shape=(jax.Sha...  48.7 us
    pallas_call x1, Pallas kernels, fused(): pl.pallas_call(store_kernel, out_shape=tuple((jax.ShapeDtypeStruct(r.shap...  2.32 us

profile of v2, /device:TPU:1, one launch (start us, length us, event | category | flops | bytes accessed | tf_op | source)
XLA Modules:
  0.0 51.7 jit_solution(9828795024147015534)
XLA Ops:
  0.6 48.7 %shard_map.120 = (f32[2,64,2048]{2,1,0:T(8,128)}, f32[64,256]{1,0:T(8,128)}, f32[64,256]{1,0:T(8,128)}, f32[64,256]{1,0:T(8,128)}) custom-call(f32[2,64,2048]{2,1,0:T(8,128)} %tracer_hbm.1, f32[64,256]{1,0:T(8,128)} %depth_hbm.1, f32[64,256]{1,0:T(8,128)} %east_hbm.1, f32[64,256]{1,0:T(8,128)} %south_hbm.1, f32[64,256]{1,0:T(8,128)} %bed_hbm.1, ...), custom_call_target="tpu_custom_call" | custom-call | tf_op jit(solution)/shard_map/pallas_call | solution.py:583
  49.3 2.3 %shard_map.121 = (f32[2,64,2048]{2,1,0:T(8,128)}, f32[64,256]{1,0:T(8,128)}, f32[64,256]{1,0:T(8,128)}, f32[64,256]{1,0:T(8,128)}) custom-call(f32[2,64,2048]{2,1,0:T(8,128)} %get-tuple-element.8.refs_0_, f32[64,256]{1,0:T(8,128)} %get-tuple-element.9.refs_1_, f32[64,256]{1,0:T(8,128)} %get-tuple-element.10.refs_2_, f32[64,256]{1,0:T(8,128)} %get-tuple-element.11.refs_3_), custom_call_target="tpu_custom_call" | custom-call | tf_op jit(solution)/shard_map/pallas_call | solution.py:625
